TPU v7x, 256 devices: a whole 4x4x8 slice. The times are simulated.
256 devices in a mesh: group: 8 (over y, core), slab: 32 (over x, z).
Axes of the slice: x: 4, y: 4, z: 8, core: 2. Of those that a mesh axis runs over, the one named last changes fastest.
Arguments:
- volume: bfloat16 [32768, 2, 384], P('slab'), may hold values from -6 to 6
- weight_tiles: bfloat16 [4, 384, 384], replicated, may hold values from 0 to 0.08984375
- ctf_table: float32 [8, 48, 384], replicated, may hold values from -1 to 1
- observed: bfloat16 [2048, 48, 2, 384], P(('group', 'slab')), may hold values from -6 to 6
- routes: int32 [2048, 48, 2], P(('group', 'slab')), may hold values from 0 to 127, all different within a row; in each aligned block of 384 rows (0 to 383, 384 to 767, ..., all dimensions but the last counted through in order) at most 12 rows name the same one
- piece_index: int32 [2048, 48, 2], P(('group', 'slab')), may hold values from 0 to 1023
- pose_index: int32 [2048], P(('group', 'slab')), may hold values from 0 to 31
- ctf_class: int32 [2048], P(('group', 'slab')), may hold values from 0 to 7
Outputs:
- back_projected: float32 [32768, 2, 384], P('slab')
- residuals: bfloat16 [2048, 48, 2, 384], P(('group', 'slab'))
Inputs may be any that keep to these rules, and one draw needn't show every extreme that they name: routes // 4 is the slab device holding the reference line, routes % 4 the tile; the two entries of a line differ; the lines of one device name each value at most 12 times, a bound that some block reaches.
All inputs are finite; a program needn't handle non-finite values.
Results may differ from a plain program's by a relative error of at most 0.012.
Values may be sent and summed in bfloat16 or wider, within the bound.
A program may use at most 64 MiB of HBM per device.

v0:
```python
import jax
import jax.numpy as jnp
from jax import lax
from jax.sharding import PartitionSpec as P

POSES = 32


def earlier_counts(onehot):
    count = onehot.shape[-2]
    lower = (
        jnp.arange(count, dtype=jnp.int32)[:, None] > jnp.arange(count, dtype=jnp.int32)[None, :]
    ).astype(jnp.bfloat16)
    return jnp.einsum(
        "nk,...kb->...nb", lower, onehot.astype(jnp.bfloat16), preferred_element_type=jnp.float32
    )


def slot_places(routes, buckets, capacity):
    flat_route = routes.reshape(-1)
    onehot = (flat_route[:, None] == jnp.arange(buckets, dtype=jnp.int32)[None, :]).astype(
        jnp.float32
    )
    earlier = earlier_counts(onehot)
    slot_rank = jnp.sum(earlier * onehot, axis=1).astype(jnp.int32)
    return flat_route * capacity + slot_rank


def on_device(
    volume, weight_tiles, ctf_table, observed, routes, piece_index, pose_index, ctf_class
):
    piece_count = volume.shape[0]
    box_len = volume.shape[2]
    tile_count = weight_tiles.shape[0]
    class_count = ctf_table.shape[0]
    image_count = observed.shape[0]
    line_count = observed.shape[1]
    owners = lax.axis_size("slab")
    buckets = owners * tile_count
    capacity = max(2, 4 * image_count * line_count // buckets)
    slot_total = buckets * capacity
    stride = piece_count + 1
    places = slot_places(routes, buckets, capacity)
    slot_ids = jnp.arange(slot_total, dtype=jnp.int32)
    matches = places[:, None] == slot_ids[None, :]
    slot_hot = matches.astype(jnp.bfloat16)
    code_base = slot_ids // capacity % tile_count * stride
    filled = jnp.sum(jnp.where(matches, piece_index.reshape(-1)[:, None] + 1, 0), axis=0)
    codes = (code_base + filled).reshape(owners, tile_count, capacity)
    item_codes = lax.all_to_all(codes, "slab", split_axis=0, concat_axis=0, tiled=True)
    tile_ids = item_codes[0, :, 0] // stride
    slot_piece = jnp.maximum(item_codes % stride - 1, 0).reshape(-1)
    piece_hot = (slot_piece[:, None] == jnp.arange(piece_count, dtype=jnp.int32)[None, :]).astype(
        jnp.bfloat16
    )
    slot_rows = jnp.dot(
        piece_hot, volume.reshape(piece_count, 2 * box_len), preferred_element_type=jnp.float32
    ).astype(jnp.bfloat16)
    slot_rows = slot_rows.reshape(item_codes.shape + (2, box_len))
    answers = lax.all_to_all(
        jnp.einsum(
            "otcrx,txy->otcry",
            slot_rows,
            weight_tiles[tile_ids],
            preferred_element_type=jnp.float32,
        ).astype(jnp.bfloat16),
        "slab",
        split_axis=0,
        concat_axis=0,
        tiled=True,
    )
    slot_values = jnp.dot(
        slot_hot, answers.reshape(slot_total, 2 * box_len), preferred_element_type=jnp.float32
    )
    slot_values = slot_values.reshape(image_count, line_count, 2, 2, box_len)
    projected = slot_values[:, :, 0] + slot_values[:, :, 1]
    wavenumber = jnp.arange(box_len).astype(jnp.float32)
    shifts = (pose_index - POSES // 2).astype(jnp.float32)
    phases = 2.0 * jnp.pi * shifts[:, None] * wavenumber[None, :] / box_len
    cos_table = jnp.cos(phases)[:, None, :]
    sin_table = jnp.sin(phases)[:, None, :]
    real_part = projected[:, :, 0] * cos_table - projected[:, :, 1] * sin_table
    imag_part = projected[:, :, 0] * sin_table + projected[:, :, 1] * cos_table
    class_onehot = (ctf_class[:, None] == jnp.arange(class_count, dtype=jnp.int32)[None, :]).astype(
        jnp.float32
    )
    ctf_lines = jnp.dot(
        class_onehot, ctf_table.reshape(class_count, -1), precision=lax.Precision.HIGHEST
    ).reshape(image_count, line_count, box_len)
    res_real = observed[:, :, 0].astype(jnp.float32) - ctf_lines * real_part
    res_imag = observed[:, :, 1].astype(jnp.float32) - ctf_lines * imag_part
    residual = jnp.stack([res_real, res_imag], axis=2).astype(jnp.bfloat16)
    weighted_real = ctf_lines * res_real
    weighted_imag = ctf_lines * res_imag
    back_real = weighted_real * cos_table + weighted_imag * sin_table
    back_imag = weighted_imag * cos_table - weighted_real * sin_table
    returned = jnp.stack([back_real, back_imag], axis=2).astype(jnp.bfloat16)
    slot_returns = jnp.broadcast_to(
        returned[:, :, None], (image_count, line_count, 2, 2, box_len)
    ).reshape(-1, 2 * box_len)
    send_buffer = jnp.einsum(
        "ms,mx->sx", slot_hot, slot_returns, preferred_element_type=jnp.float32
    ).astype(jnp.bfloat16)
    send_buffer = send_buffer.reshape(owners, tile_count, capacity, 2, box_len)
    received = lax.all_to_all(send_buffer, "slab", split_axis=0, concat_axis=0, tiled=True)
    back_rows = jnp.einsum(
        "otcry,txy->otcrx", received, weight_tiles, preferred_element_type=jnp.float32
    )
    target_piece = jnp.maximum(item_codes % stride - 1, 0).reshape(-1)
    target_hot = (
        jnp.arange(piece_count, dtype=jnp.int32)[:, None] == target_piece[None, :]
    ).astype(jnp.float32)
    partial_sum = jnp.dot(
        target_hot, back_rows.reshape(-1, 2 * box_len), precision=lax.Precision.HIGHEST
    ).reshape(piece_count, 2, box_len)
    back_projected = lax.psum(partial_sum.astype(jnp.bfloat16), "group").astype(jnp.float32)
    return (back_projected, residual)


def solution(mesh):
    in_specs = (
        P("slab", None, None),
        P(),
        P(),
        P(("group", "slab"), None, None, None),
        P(("group", "slab"), None, None),
        P(("group", "slab"), None, None),
        P(("group", "slab")),
        P(("group", "slab")),
    )
    out_specs = (P("slab", None, None), P(("group", "slab"), None, None, None))
    return jax.shard_map(
        on_device, mesh=mesh, in_specs=in_specs, out_specs=out_specs, check_vma=False
    )
```

profile of v0, /device:TPU:17, one launch (start us, length us, event | category | flops | bytes accessed | tf_op | source)
XLA Modules:
  0.0 294.9 jit_solution(6034027468822676551)
XLA Ops:
  7.2 0.0 copy-start
  7.2 0.9 broadcast_add_fusion
  8.0 0.1 copy.92
  8.2 0.1 add.89
  8.3 0.8 copy.91
  9.2 0.1 reshape.223
  9.3 0.4 fusion.30
  9.8 0.6 copy-done.9
  10.3 0.6 select_reduce_fusion
  10.9 0.1 reduce_sum.22
  11.0 0.8 fusion.36
  11.8 11.0 %all-to-all-start = ((s32[32,4,12]{2,1,0:T(4,128)}), s32[32,4,12]{2,1,0:T(4,128)S(1)}, u32[]{:S(2)}, u32[]{:S(2)}) async-start(s32[32,4,12]{2,1,0:T(4,128)} %fusion.36), calls=%async_computation | async-start | bytes 131072 | tf_op jit(solution)/shard_map/all_to_all | solution.py:50
  22.9 0.0 copy-done.4
  22.9 1.5 copy.118
  24.3 7.4 %all-to-all-done = s32[32,4,12]{2,1,0:T(4,128)S(1)} async-done(((s32[32,4,12]{2,1,0:T(4,128)}), s32[32,4,12]{2,1,0:T(4,128)S(1)}, u32[]{:S(2)}, u32[]{:S(2)}) %all-to-all-start) | async-done | bytes 6176 | tf_op jit(solution)/shard_map/all_to_all | solution.py:50
  31.7 0.1 fusion.38
  31.8 0.1 eq.101
  31.9 0.1 divide_reduce_fusion
  32.1 0.1 fusion.48
  32.2 0.3 copy-done.11
  32.5 5.6 %fusion.9 = bf16[1536,768]{1,0:T(8,128)(2,1)} fusion(bf16[1024,768]{1,0:T(8,128)(2,1)} %bitcast.116, s32[1536]{0:T(1024)S(1)} %eq.101), kind=kOutput, calls=%fused_computation.14 | convolution fusion | flops 2418671616 | bytes 3938304 | tf_op jit(solution)/shard_map/dot_general | solution.py:56
  38.1 4.7 %reshape.226 = bf16[32,4,12,2,384]{4,3,2,1,0:T(2,128)(2,1)S(1)} reshape(bf16[1536,768]{1,0:T(8,128)(2,1)} %fusion.9) | data formatting | bytes 4718592 | tf_op jit(solution)/shard_map/reshape | solution.py:59
  42.8 1.7 gather_fusion
  44.6 2.9 convert_bitcast_fusion
  47.5 3.2 %copy.98 = bf16[32,4,12,2,384]{4,3,2,1,0:T(2,128)(2,1)} copy(bf16[32,4,12,2,384]{4,0,3,2,1:T(8,128)(2,1)S(1)} %convert_bitcast_fusion) | data formatting | bytes 4718592 | tf_op jit(solution)/shard_map/convert_element_type | solution.py:66
  50.7 4.2 %all-to-all-start.1 = ((bf16[32,4,12,2,384]{4,3,2,1,0:T(2,128)(2,1)}), bf16[32,4,12,2,384]{4,3,2,1,0:T(2,128)(2,1)S(1)}, u32[]{:S(2)}, u32[]{:S(2)}) async-start(bf16[32,4,12,2,384]{4,3,2,1,0:T(2,128)(2,1)} %copy.98), calls=%async_computation.1 | async-start | bytes 4718592 | tf_op jit(solution)/shard_map/all_to_all | solution.py:60
  54.9 0.2 all-reduce.2.cloned.1.call-start
  55.1 0.8 convert_element_type.73
  56.0 1.0 copy.95
  57.0 0.0 copy-done.8
  57.0 0.7 convert_multiply_fusion
  57.7 0.7 fusion.41
  58.4 2.4 fusion.44
  60.9 3.3 %fusion.50 = (bf16[8,48,1,384]{3,2,1,0:T(2,128)(2,1)}, bf16[8,48,1,384]{3,2,1,0:T(2,128)(2,1)}) fusion(bf16[8,48,2,384]{3,2,1,0:T(2,128)(2,1)} %param.11), kind=kLoop, calls=%fused_computation.86 | loop fusion | bytes 1179648 | tf_op jit(solution)/shard_map/slice | solution.py:90
  64.2 1.8 fusion.5
  65.9 43.5 %all-to-all-done.1 = bf16[32,4,12,2,384]{4,3,2,1,0:T(2,128)(2,1)S(1)} async-done(((bf16[32,4,12,2,384]{4,3,2,1,0:T(2,128)(2,1)}), bf16[32,4,12,2,384]{4,3,2,1,0:T(2,128)(2,1)S(1)}, u32[]{:S(2)}, u32[]{:S(2)}) %all-to-all-start.1) | async-done | bytes 2359328 | tf_op jit(solution)/shard_map/all_to_all | solution.py:60
  109.4 1.9 copy.119
  111.3 2.8 copy.99
  114.2 3.6 %fusion.6 = f32[8,48,2,2,384]{4,0,1,3,2:T(8,128)S(1)} fusion(bf16[2,384,1536,1,1]{2,1,3,0,4:T(8,128)(2,1)S(1)} %bitcast.114, pred[8,48,2,1536,1]{3,1,2,0,4:T(8,128)(4,1)} %fusion.5), kind=kOutput, calls=%fused_computation.11 | convolution fusion | flops 1811939328 | bytes 5898240 | tf_op jit(solution)/shard_map/dot_general | solution.py:72
  117.8 0.0 copy-start.1
  117.8 0.1 fusion.27
  118.0 0.9 copy-done.1
  118.9 0.2 copy-done.2
  119.0 0.2 copy-done.3
  119.2 1.2 convert_bitcast_fusion.2
  120.5 0.2 fusion.31
  120.7 0.1 pad_maximum_fusion
  120.8 0.6 copy.103
  121.4 0.6 broadcast_in_dim.16
  122.0 0.2 copy.120
  122.3 3.9 %fusion.8 = bf16[1536,768]{1,0:T(8,128)(2,1)} fusion(bf16[768,768]{1,0:T(8,128)(2,1)S(1)} %bitcast.117, s32[768]{0:T(1024)S(1)} %copy-done.10), kind=kOutput, calls=%fused_computation.13 | convolution fusion | flops 1814298624 | bytes 3542016 | tf_op jit(solution)/shard_map/ms,mx->sx/dot_general | solution.py:101
  126.2 4.7 %reshape.229 = bf16[32,4,12,2,384]{4,3,2,1,0:T(2,128)(2,1)S(1)} reshape(bf16[1536,768]{1,0:T(8,128)(2,1)} %fusion.8) | data formatting | bytes 4718592 | tf_op jit(solution)/shard_map/reshape | solution.py:104
  130.8 59.8 %all_to_all.15 = bf16[32,4,12,2,384]{4,3,2,1,0:T(2,128)(2,1)S(1)} all-to-all(bf16[32,4,12,2,384]{4,3,2,1,0:T(2,128)(2,1)S(1)} %reshape.229), channel_id=1, replica_groups=mesh['group'=8,'slab'=32] {'slab'}, dimensions={0} | all-to-all | bytes 4718592 | tf_op jit(solution)/shard_map/all_to_all | solution.py:105
  190.7 1.7 fusion.18
  192.4 3.6 %copy.105 = f32[32,4,12,2,384]{4,3,2,1,0:T(2,128)S(1)} copy(f32[32,4,12,2,384]{4,0,3,2,1:T(8,128)S(1)} %fusion.18) | data formatting | bytes 9437184 | tf_op jit(solution)/shard_map/otcry,txy->otcrx/transpose | solution.py:106
  196.0 2.5 copy.121
  198.5 6.1 %copy.114 = f32[768,1536]{1,0:T(8,128)} copy(f32[768,1536]{0,1:T(8,128)} %bitcast.109) | data formatting | bytes 9437184 | tf_op jit(solution)/shard_map/dot_general | solution.py:113
  204.6 0.0 copy-done.12
  204.6 12.8 %fusion.23 = bf16[1024,2,384]{2,0,1:T(8,128)(2,1)} fusion(f32[2,384,1536]{2,1,0:T(8,128)} %bitcast.112, s32[1536]{0:T(1024)S(1)} %copy-done.12), kind=kOutput, calls=%fused_computation.26 | convolution fusion | flops 14497873920 | bytes 6297600 | tf_op jit(solution)/shard_map/dot_general | solution.py:113
  217.4 0.0 all-reduce.2.cloned.1.call-update
  217.4 0.1 pad_maximum_fusion.1
  217.5 1.4 copy.108
  218.9 64.5 %all-reduce.2.cloned.1.call-done = bf16[1024,2,384]{2,0,1:T(8,128)(2,1)} async-done(((bf16[1024,2,384]{2,0,1:T(8,128)(2,1)}), bf16[1024,2,384]{2,0,1:T(8,128)(2,1)}) %all-reduce.2.cloned.1.call-update) | async-done | bytes 1572880 | tf_op jit(solution)/shard_map/psum | solution.py:116
  283.4 4.7 %copy.107 = f32[1024,2,384]{2,1,0:T(2,128)} copy(bf16[1024,2,384]{2,0,1:T(8,128)(2,1)} %all-reduce.2.cloned.1.call-done) | data formatting | bytes 4718592
  (23 shorter events, 0.1 us)
Async XLA Ops:
  7.2 35.7 %copy-start = (bf16[4,384,384]{2,1,0:T(8,128)(2,1)S(1)}, bf16[4,384,384]{2,1,0:T(8,128)(2,1)}, u32[]{:S(2)}) copy-start(bf16[4,384,384]{2,1,0:T(8,128)(2,1)} %param.9) | copy-start | bytes 3538948
  7.2 15.7 %copy-start.4 = (bf16[1024,2,384]{2,1,0:T(2,128)(2,1)S(1)}, bf16[1024,2,384]{2,1,0:T(2,128)(2,1)}, u32[]{:S(2)}) copy-start(bf16[1024,2,384]{2,1,0:T(2,128)(2,1)} %param.8) | copy-start | bytes 4718596
  9.7 0.6 copy-start.9
  11.8 19.9 %all-to-all-start = ((s32[32,4,12]{2,1,0:T(4,128)}), s32[32,4,12]{2,1,0:T(4,128)S(1)}, u32[]{:S(2)}, u32[]{:S(2)}) async-start(s32[32,4,12]{2,1,0:T(4,128)} %fusion.36), calls=%async_computation | async-start | bytes 131072 | tf_op jit(solution)/shard_map/all_to_all | solution.py:50
  31.9 0.6 copy-start.11
  50.7 6.3 %copy-start.8 = (s32[8,48,2]{1,2,0:T(2,128)S(1)}, s32[8,48,2]{1,2,0:T(2,128)}, u32[]{:S(2)}) copy-start(s32[8,48,2]{1,2,0:T(2,128)} %param.12) | copy-start | bytes 9220
  50.7 58.8 %all-to-all-start.1 = ((bf16[32,4,12,2,384]{4,3,2,1,0:T(2,128)(2,1)}), bf16[32,4,12,2,384]{4,3,2,1,0:T(2,128)(2,1)S(1)}, u32[]{:S(2)}, u32[]{:S(2)}) async-start(bf16[32,4,12,2,384]{4,3,2,1,0:T(2,128)(2,1)} %copy.98), calls=%async_computation.1 | async-start | bytes 4718592 | tf_op jit(solution)/shard_map/all_to_all | solution.py:60
  54.9 228.5 %all-reduce.2.cloned.1.call-start = ((), (), s32[]{:S(2)}) async-start(), calls=%async_computation.3 | async-start | bytes 3145728 | tf_op jit(solution)/shard_map/psum | solution.py:116
  117.8 1.1 copy-start.1
  117.8 1.2 copy-start.2
  117.8 1.4 copy-start.3
  117.8 1.4 copy-start.7
  121.4 0.9 copy-start.10
  198.5 6.1 %copy-start.12 = (s32[1536]{0:T(1024)S(1)}, s32[1536]{0:T(1024)}, u32[]{:S(2)}) copy-start(s32[1536]{0:T(1024)} %copy-done.11) | copy-start | bytes 18436
  204.6 12.8 %copy-start.5 = (bf16[8,48,1,384]{3,0,1,2:T(8,128)(2,1)S(1)}, bf16[8,48,1,384]{3,0,1,2:T(8,128)(2,1)}, u32[]{:S(2)}) copy-start(bf16[8,48,1,384]{3,0,1,2:T(8,128)(2,1)} %get-tuple-element.14) | copy-start | bytes 884740
  204.6 12.8 %copy-start.6 = (bf16[8,48,1,384]{3,0,1,2:T(8,128)(2,1)S(1)}, bf16[8,48,1,384]{3,0,1,2:T(8,128)(2,1)}, u32[]{:S(2)}) copy-start(bf16[8,48,1,384]{3,0,1,2:T(8,128)(2,1)} %get-tuple-element.20) | copy-start | bytes 884740
Sparse Core Ops, SparseCore 0:
  217.5 65.8 all-reduce.1
where the time goes:
time: 299 us; the launch traced here: 295 us
  waiting for transfers between devices  115 us (38%)
  blocking collectives  59.8 us (20%)
  local copies, waits for them, and re-layouts  49.1 us (16%)
  matrix products  33.3 us (11%)
  starting transfers between devices  15.4 us (5%)
  between operations  14.4 us (5%)
  other arithmetic  7.43 us (2%)
    psum x1, waiting for transfers between devices, on_device(): lax.psum(partial_sum.astype(jnp.bfloat16), 'group').astype(jnp.float32)  64.5 us
    all_to_all x1, blocking collectives, on_device(): lax.all_to_all(send_buffer, 'slab', split_axis=0, concat_axis=0, tiled=True)  59.8 us
    all_to_all x1, waiting for transfers between devices, on_device(): lax.all_to_all(jnp.einsum('otcrx,txy->otcry', slot_rows, weight_tiles[til...  43.5 us
    unnamed x33, local copies, waits for them, and re-layouts  15.2 us
    dot_general x1, matrix products, on_device(): jnp.dot(target_hot, back_rows.reshape(-1, 2 * box_len), precision=lax.Pre...  12.8 us
    all_to_all x1, starting transfers between devices, on_device(): lax.all_to_all(codes, 'slab', split_axis=0, concat_axis=0, tiled=True)  11 us
    all_to_all x1, waiting for transfers between devices, on_device(): lax.all_to_all(codes, 'slab', split_axis=0, concat_axis=0, tiled=True)  7.39 us
    dot_general x1, local copies, waits for them, and re-layouts, on_device(): jnp.dot(target_hot, back_rows.reshape(-1, 2 * box_len), precision=lax.Pre...  6.07 us
  transfers between devices with their start and end apart: 3, of which 3 were waited for; matrix products, arithmetic and copies ran while one was open for 5% of the time, Pallas kernels for 0%

commit v1 on v0

v1 whole, which is shorter than its diff:
```python
import functools

import jax
import jax.numpy as jnp
from jax import lax
from jax.experimental import pallas as pl
from jax.experimental.pallas import tpu as pltpu
from jax.sharding import PartitionSpec as P

MESH = pl.DeviceIdType.MESH
POSES = 32
CORES = 2
BATCHES = 4
BF = jnp.bfloat16
F32 = jnp.float32
NT = (((1,), (1,)), ((), ()))


def mm(a, b):
    return jnp.dot(a, b, preferred_element_type=F32)


def iota(shape, axis):
    return lax.broadcasted_iota(jnp.int32, shape, axis)


def kernel(
    cfg,
    pose_ref, cls_ref, req_ref, vol_ref, w_ref, ctf_ref, obs_ref,
    back_ref, res_ref,
    code_out, code_in, code_rows, hot, send1, recv1, pick, place, proj, ret, send2, recv2, rows_back, total,
    core_out, core_in, y_out, y_in, result,
    code_ss, code_rs, ss1, rs1, ss2, rs2, core_ss, core_rs, y_ss, y_rs, ag_ss, ag_rs, sib_ss, sib_rs,
):
    nx, nz, ny, tiles, cap, lines = cfg
    slabs = nx * nz
    groups = ny * CORES
    per = slabs // BATCHES
    chunk = tiles * cap
    rows = per * chunk
    items = req_ref.shape[1]
    pieces, width = vol_ref.shape
    box = width // 2
    shard = pieces // groups
    images = items // lines

    slab, group = lax.axis_index("slab"), lax.axis_index("group")
    my_x, my_z = slab // nz, slab % nz
    my_y, core = group // CORES, group % CORES
    sibling = {"group": my_y * CORES + 1 - core}

    def partner(k, sign):
        step = k % nz
        dz = (step % 2) * ((step + 1) // 2) + (1 - step % 2) * (nz - step // 2)
        dx = k // nz
        x = (my_x + nx + sign * dx) % nx
        z = (my_z + 2 * nz + sign * dz) % nz
        return {"slab": x * nz + z}

    def y_peer(dy):
        return {"group": (my_y + dy) % ny * CORES + core}

    barrier = pltpu.get_barrier_semaphore()

    def greet(k, carry):
        pl.semaphore_signal(barrier, inc=1, device_id=partner(k, 1), device_id_type=MESH)
        return carry

    lax.fori_loop(1, slabs, greet, 0)
    pl.semaphore_signal(barrier, inc=1, device_id=sibling, device_id_type=MESH)
    for dy in range(1, ny):
        pl.semaphore_signal(barrier, inc=1, device_id=y_peer(dy), device_id_type=MESH)

    req = req_ref[...]
    req = jnp.concatenate([req[0:1], req[1:2]], axis=1)
    bucket, piece = req >> 10, req & 1023
    tile, owner = bucket % tiles, bucket // tiles
    dx = (owner // nz + nx - my_x) % nx
    dz = (owner % nz + nz - my_z) % nz
    step = jnp.maximum(jnp.where(dz <= nz // 2, 2 * dz - 1, 2 * (nz - dz)), 0)
    server = dx * nz + step
    both = 2 * items
    own = iota((slabs * tiles, both), 0) == server * tiles + tile
    before = (iota((both, both), 0) < iota((both, both), 1)).astype(F32).astype(BF)
    earlier = mm(own.astype(F32).astype(BF), before)
    rank = jnp.sum(jnp.where(own, earlier, 0.0), axis=0, keepdims=True).astype(jnp.int32)
    seat = tile * cap + rank
    spot = server * chunk + seat
    to_server = (iota((slabs, both), 0) == server).astype(F32).astype(BF)
    at_seat = iota((128, both), 0) == seat
    low = jnp.where(at_seat, (piece & 31).astype(F32), 0.0).astype(BF)
    high = jnp.where(at_seat, (piece >> 5).astype(F32), 0.0).astype(BF)
    codes = lax.dot_general(to_server, low, NT, preferred_element_type=F32)
    codes = codes + 32.0 * lax.dot_general(to_server, high, NT, preferred_element_type=F32)
    codes = codes.astype(jnp.int32)
    for k in range(slabs):
        code_out[k] = codes[k : k + 1]
    code_in[0] = codes[0:1]

    def code_copy(k):
        return pltpu.make_async_remote_copy(
            src_ref=code_out.at[k], dst_ref=code_in.at[k], send_sem=code_ss.at[k], recv_sem=code_rs.at[k],
            device_id=partner(k, 1), device_id_type=MESH,
        )

    def answer_copy(k):
        return pltpu.make_async_remote_copy(
            src_ref=send1.at[k], dst_ref=recv1.at[k], send_sem=ss1.at[k], recv_sem=rs1.at[k],
            device_id=partner(k, -1), device_id_type=MESH,
        )

    def return_copy(k):
        return pltpu.make_async_remote_copy(
            src_ref=send2.at[k], dst_ref=recv2.at[k], send_sem=ss2.at[k], recv_sem=rs2.at[k],
            device_id=partner(k, 1), device_id_type=MESH,
        )

    def each(first, last, action):
        def body(k, carry):
            action(k)
            return carry

        lax.fori_loop(first, last, body, 0)

    pl.semaphore_wait(barrier, slabs - 1 + ny)
    each(1, slabs, lambda k: code_copy(k).start())

    spot0, spot1 = spot[:, :items], spot[:, items:]
    diagonal = iota((items, items), 0) == iota((items, items), 1)
    col0 = jnp.sum(jnp.where(diagonal, spot0.astype(F32), 0.0), axis=1, keepdims=True).astype(jnp.int32)
    col1 = jnp.sum(jnp.where(diagonal, spot1.astype(F32), 0.0), axis=1, keepdims=True).astype(jnp.int32)
    for b in range(BATCHES):
        across = iota((items, rows), 1) + b * rows
        pick[b] = ((across == col0) | (across == col1)).astype(F32).astype(BF)
        down = iota((rows, items), 0) + b * rows
        place[b] = ((down == spot0) | (down == spot1)).astype(F32).astype(BF)

    row_tile = iota((rows, box), 0) % chunk // cap

    def serve(b, carry):
        for c in range(per):
            k = b * per + c

            @pl.when(k > 0)
            def _():
                code_copy(k).wait_recv()

        line = jnp.zeros((1, rows), F32)
        for c in range(per):
            code = code_in[b * per + c].astype(F32)
            eye = iota((chunk, 128), 0) == iota((chunk, 128), 1)
            col = jnp.sum(jnp.where(eye, code, 0.0), axis=1, keepdims=True)
            spread = iota((chunk, rows), 0) + c * chunk == iota((chunk, rows), 1)
            line = line + jnp.sum(jnp.where(spread, col, 0.0), axis=0, keepdims=True)
            hot[c * chunk : (c + 1) * chunk] = (iota((chunk, pieces), 1) == col.astype(jnp.int32)).astype(F32).astype(BF)
        code_rows[b] = line.astype(jnp.int32)
        fetched = mm(hot[...], vol_ref[...])
        for part in range(2):
            half = fetched[:, part * box : (part + 1) * box]
            answer = jnp.zeros((rows, box), F32)
            for t in range(tiles):
                answer = answer + mm(jnp.where(row_tile == t, half, 0.0).astype(BF), w_ref[t])
            send1[pl.ds(b * per, per), :, part * box : (part + 1) * box] = answer.astype(BF).reshape(per, chunk, box)
        for c in range(per):
            k = b * per + c

            @pl.when(k > 0)
            def _():
                answer_copy(k).start()

        return carry

    lax.fori_loop(0, BATCHES, serve, 0)
    recv1[0] = send1[0]

    number = iota((images, box), 0)
    shift = jnp.zeros((images, box), F32)
    for i in range(images):
        shift = jnp.where(number == i, (pose_ref[i] - POSES // 2).astype(F32), shift)
    phases = 2.0 * jnp.pi * shift * iota((images, box), 1).astype(F32) / box
    cos_table, sin_table = jnp.cos(phases), jnp.sin(phases)

    proj[...] = jnp.zeros_like(proj)

    def collect(b, carry):
        for c in range(per):
            k = b * per + c

            @pl.when(k > 0)
            def _():
                answer_copy(k).wait_recv()

        proj[...] += mm(pick[b], recv1[pl.ds(b * per, per)].reshape(rows, width))
        return carry

    lax.fori_loop(0, BATCHES, collect, 0)

    for i in range(images):
        at = slice(i * lines, (i + 1) * lines)
        real, imag = proj[at, :box], proj[at, box:]
        cos, sin = cos_table[i : i + 1], sin_table[i : i + 1]
        ctf = ctf_ref[cls_ref[i]]
        res_real = obs_ref[at, :box].astype(F32) - ctf * (real * cos - imag * sin)
        res_imag = obs_ref[at, box:].astype(F32) - ctf * (real * sin + imag * cos)
        res_ref[at, :box] = res_real.astype(BF)
        res_ref[at, box:] = res_imag.astype(BF)
        real, imag = ctf * res_real, ctf * res_imag
        ret[at, :box] = (real * cos + imag * sin).astype(BF)
        ret[at, box:] = (imag * cos - real * sin).astype(BF)

    def give_back(b, carry):
        filled = mm(place[b], ret[...]).astype(BF)
        send2[pl.ds(b * per, per)] = filled.reshape(per, chunk, width)
        for c in range(per):
            k = b * per + c

            @pl.when(k > 0)
            def _():
                return_copy(k).start()

        return carry

    lax.fori_loop(0, BATCHES, give_back, 0)
    recv2[0] = send2[0]
    total[...] = jnp.zeros_like(total)

    def add_shard(b, m):
        at_piece = iota((shard, rows), 0) + m * shard == code_rows[b]
        total[m] += mm(at_piece.astype(F32).astype(BF), rows_back[...])

    def absorb(b, carry):
        for c in range(per):
            k = b * per + c

            @pl.when(k > 0)
            def _():
                return_copy(k).wait_recv()

        got = recv2[pl.ds(b * per, per)].reshape(rows, width).astype(F32)
        for part in range(2):
            half = got[:, part * box : (part + 1) * box]
            back = jnp.zeros((rows, box), F32)
            for t in range(tiles):
                masked = jnp.where(row_tile == t, half, 0.0).astype(BF)
                back = back + lax.dot_general(masked, w_ref[t], NT, preferred_element_type=F32)
            rows_back[:, part * box : (part + 1) * box] = back.astype(BF)

        @pl.when(b < BATCHES - 1)
        def _():
            each(0, groups, lambda m: add_shard(b, m))

        return carry

    lax.fori_loop(0, BATCHES, absorb, 0)

    def core_copy(d):
        return pltpu.make_async_remote_copy(
            src_ref=core_out.at[d], dst_ref=core_in.at[d], send_sem=core_ss.at[d], recv_sem=core_rs.at[d],
            device_id=sibling, device_id_type=MESH,
        )

    def y_copy(d):
        return pltpu.make_async_remote_copy(
            src_ref=y_out.at[d], dst_ref=y_in.at[d], send_sem=y_ss.at[d], recv_sem=y_rs.at[d],
            device_id=y_peer(d), device_id_type=MESH,
        )

    def spread_copy(d):
        return pltpu.make_async_remote_copy(
            src_ref=result.at[group], dst_ref=result.at[group], send_sem=ag_ss.at[d], recv_sem=ag_rs.at[d],
            device_id=y_peer(d), device_id_type=MESH,
        )

    def sibling_copy(d):
        m = (my_y + ny - d) % ny * CORES + core
        return pltpu.make_async_remote_copy(
            src_ref=result.at[m], dst_ref=result.at[m], send_sem=sib_ss.at[d], recv_sem=sib_rs.at[d],
            device_id=sibling, device_id_type=MESH,
        )

    order = [*range(1, ny), 0]
    last = BATCHES - 1
    for d in order:
        m = (my_y + d) % ny * CORES + 1 - core
        add_shard(last, m)
        core_out[d] = total[m].astype(BF)
        core_copy(d).start()
    for d in order:
        add_shard(last, (my_y + d) % ny * CORES + core)
    for d in order:
        m = (my_y + d) % ny * CORES + core
        core_copy(d).wait_recv()
        total[m] += core_in[d].astype(F32)
        if d > 0:
            y_out[d] = total[m].astype(BF)
            y_copy(d).start()
    for d in range(1, ny):
        y_copy(d).wait_recv()
        total[group] += y_in[d].astype(F32)
    result[group] = total[group].astype(BF)
    for d in range(1, ny):
        spread_copy(d).start()
    sibling_copy(0).start()
    for d in range(1, ny):
        spread_copy(d).wait_recv()
        sibling_copy(d).start()
    for d in range(ny):
        sibling_copy(d).wait_recv()
    back_ref[...] = result[...].reshape(pieces, width)

    def drain(k):
        code_copy(k).wait_send()
        answer_copy(k).wait_send()
        return_copy(k).wait_send()

    each(1, slabs, drain)
    for d in range(ny):
        core_copy(d).wait_send()
        sibling_copy(d).wait_send()
        if d > 0:
            y_copy(d).wait_send()
            spread_copy(d).wait_send()


def on_device(nx, nz, ny, volume, weight_tiles, ctf_table, observed, routes, piece_index, pose_index, ctf_class):
    pieces, _, box = volume.shape
    images, lines = observed.shape[:2]
    items = images * lines
    tiles = weight_tiles.shape[0]
    slabs, groups = nx * nz, ny * CORES
    cap = max(2, 4 * items // (slabs * tiles))
    per = slabs // BATCHES
    chunk = tiles * cap
    rows = per * chunk
    width = 2 * box
    shard = pieces // groups
    requests = (routes * 1024 + piece_index).transpose(2, 0, 1).reshape(2, items)
    vmem, smem = pl.BlockSpec(memory_space=pltpu.VMEM), pl.BlockSpec(memory_space=pltpu.SMEM)
    dma = pltpu.SemaphoreType.DMA
    back, residual = pl.pallas_call(
        functools.partial(kernel, (nx, nz, ny, tiles, cap, lines)),
        out_shape=(jax.ShapeDtypeStruct((pieces, width), BF), jax.ShapeDtypeStruct((items, width), BF)),
        in_specs=[smem, smem, vmem, vmem, vmem, vmem, vmem],
        out_specs=(vmem, vmem),
        scratch_shapes=[
            pltpu.VMEM((slabs, 1, 128), jnp.int32),
            pltpu.VMEM((slabs, 1, 128), jnp.int32),
            pltpu.VMEM((BATCHES, 1, rows), jnp.int32),
            pltpu.VMEM((rows, pieces), BF),
            pltpu.VMEM((slabs, chunk, width), BF),
            pltpu.VMEM((slabs, chunk, width), BF),
            pltpu.VMEM((BATCHES, items, rows), BF),
            pltpu.VMEM((BATCHES, rows, items), BF),
            pltpu.VMEM((items, width), F32),
            pltpu.VMEM((items, width), BF),
            pltpu.VMEM((slabs, chunk, width), BF),
            pltpu.VMEM((slabs, chunk, width), BF),
            pltpu.VMEM((rows, width), BF),
            pltpu.VMEM((groups, shard, width), F32),
            pltpu.VMEM((ny, shard, width), BF),
            pltpu.VMEM((ny, shard, width), BF),
            pltpu.VMEM((ny, shard, width), BF),
            pltpu.VMEM((ny, shard, width), BF),
            pltpu.VMEM((groups, shard, width), BF),
            *[dma((slabs,))] * 6,
            *[dma((ny,))] * 8,
        ],
        compiler_params=pltpu.CompilerParams(collective_id=0, has_side_effects=True, vmem_limit_bytes=56 * 2**20),
    )(
        pose_index, ctf_class, requests, volume.reshape(pieces, width), weight_tiles, ctf_table,
        observed.reshape(items, width),
    )
    return back.reshape(pieces, 2, box).astype(F32), residual.reshape(images, lines, 2, box)


def solution(mesh):
    slabs, groups = mesh.shape["slab"], mesh.shape["group"]
    nz = 8 if slabs % 8 == 0 else 2
    by_device = ("group", "slab")
    return jax.shard_map(
        functools.partial(on_device, slabs // nz, nz, groups // CORES),
        mesh=mesh,
        in_specs=(
            P("slab", None, None), P(), P(), P(by_device, None, None, None), P(by_device, None, None),
            P(by_device, None, None), P(by_device), P(by_device),
        ),
        out_specs=(P("slab", None, None), P(by_device, None, None, None)),
        check_vma=False,
    )
```

time: 299 us -> 171 us (0.57)
  the two profiles are of different devices: /device:TPU:17 before, /device:TPU:33 now
where the time goes in v1:
time: 171 us
  Pallas kernels  157 us (92%)
  local copies, waits for them, and re-layouts  12.7 us (7%)
    pallas_call x1, Pallas kernels, on_device(): pl.pallas_call(functools.partial(kernel, (nx, nz, ny, tiles, cap, lines))...  157 us
    unnamed x2, local copies, waits for them, and re-layouts  4.82 us
    convert_element_type x1, local copies, waits for them, and re-layouts, on_device(): back.reshape(pieces, 2, box).astype(F32)  4.72 us

profile of v1, /device:TPU:33, one launch (start us, length us, event | category | flops | bytes accessed | tf_op | source)
XLA Modules:
  0.0 170.9 jit_solution(4139842282333620593)
XLA Ops:
  0.6 0.7 add_bitcast_fusion
  1.4 0.7 reshape.19.req_ref
  2.0 2.0 %copy.12 = bf16[48,8,2,384]{3,1,2,0:T(8,128)(2,1)} copy(bf16[48,8,2,384]{3,2,1,0:T(2,128)(2,1)} %bitcast.10) | data formatting | bytes 1179648
  4.0 2.9 %copy.11 = bf16[128,8,2,384]{3,1,2,0:T(8,128)(2,1)} copy(bf16[128,8,2,384]{3,2,1,0:T(2,128)(2,1)} %bitcast.9) | data formatting | bytes 3145728
  6.8 156.8 %shard_map.95 = (bf16[1024,768]{1,0:T(8,128)(2,1)}, bf16[384,768]{1,0:T(8,128)(2,1)}) custom-call(s32[8]{0:T(128)} %pose_ref.1, s32[8]{0:T(128)} %cls_ref.1, s32[2,384]{1,0:T(2,128)} %reshape.19.req_ref, bf16[1024,768]{1,0:T(8,128)(2,1)} %bitcast.7, bf16[4,384,384]{2,1,0:T(8,128)(2,1)} %w_ref.1, f32[8,48,384]{2,1,0:T(8,128)} %ctf_ref.1, bf16[384,768]{1,0:T(8,128)(2,1)} %bitcast.8), custom_call_target="tpu_custom_call" | custom-call | tf_op jit(solution)/shard_map/pallas_call | solution.py:340
  163.7 2.5 %reshape.22 = bf16[8,48,2,384]{3,2,1,0:T(2,128)(2,1)} reshape(bf16[384,768]{1,0:T(8,128)(2,1)} %get-tuple-element.5) | data formatting | bytes 1179648 | tf_op jit(solution)/shard_map/reshape | solution.py:373
  166.2 4.7 %reshape.23 = f32[1024,2,384]{2,1,0:T(2,128)} reshape(bf16[1024,768]{1,0:T(8,128)(2,1)} %get-tuple-element.4) | data formatting | bytes 4718592 | tf_op jit(solution)/shard_map/convert_element_type | solution.py:373
  (1 shorter events, 0.0 us)

commit v2 on v1

v2 whole, which is shorter than its diff:
```python
import functools

import jax
import jax.numpy as jnp
from jax import lax
from jax.experimental import pallas as pl
from jax.experimental.pallas import tpu as pltpu
from jax.sharding import PartitionSpec as P

MESH = pl.DeviceIdType.MESH
POSES = 32
CORES = 2
BATCHES = 4
PARTS = 4
STEPS = 8
TOGETHER = 2
BF = jnp.bfloat16
F32 = jnp.float32
NT = (((1,), (1,)), ((), ()))


def mm(a, b):
    return jnp.dot(a, b, preferred_element_type=F32)


def iota(shape, axis):
    return lax.broadcasted_iota(jnp.int32, shape, axis)


def kernel(
    cfg,
    pose_ref, cls_ref, req_ref, vol_ref, w_ref, ctf_ref, obs_ref,
    back_ref, res_ref,
    held, code_out, code_in, sum_out, sum_in, code_rows, hot, send1, recv1, pick, place, proj, ret, send2, recv2, rows_back, total,
    chain_out, chain_in, root_in, result,
    half_ss, half_rs, share_ss, share_rs, code_ss, code_rs, sum_ss, sum_rs, ss1, rs1, ss2, rs2, chain_ss, chain_rs, root_rs, up_ss, down_ss, y_rs, sib_ss, sib_rs,
):
    nx, nz, ny, tiles, cap, lines = cfg
    slabs = nx * nz
    per = slabs // BATCHES
    chunk = tiles * cap
    rows = per * chunk
    items = req_ref.shape[1]
    part_rows, width = vol_ref.shape[1:]
    pieces = ny * PARTS * part_rows
    box = width // 2
    sum_rows = pieces // STEPS
    rows_added = TOGETHER * sum_rows
    images = items // lines

    slab, group = lax.axis_index("slab"), lax.axis_index("group")
    my_x, my_z = slab // nz, slab % nz
    my_y, core = group // CORES, group % CORES
    sibling = {"group": my_y * CORES + 1 - core}

    near = nz // 4

    def at(x, z, c):
        return {"slab": (my_x + nx + x) % nx * nz + (my_z + 2 * nz + z) % nz, "group": my_y * CORES + (core + c) % CORES}

    def two_ways(j):
        return j % 2 * ((j + 1) // 2) - (1 - j % 2) * (j // 2)

    def server(k, sign):
        j = k % nz
        other = j // (2 * near + 1)
        z = two_ways(j - other * (2 * near + 1))
        return at(sign * ((k // nz + j) % nx), sign * z, other)

    def plane_at(x, y, c):
        return {
            "slab": (my_x + nx + x) % nx * nz + my_z,
            "group": (my_y + ny + y) % ny * CORES + (core + c) % CORES,
        }

    def owner(k, sign):
        m = k % (nx * ny)
        return plane_at(sign * (m % nx), sign * ((m // nx + m % nx) % ny), k // (nx * ny))

    def z_peer(d):
        return {"slab": my_x * nz + (my_z + nz + d) % nz}

    def y_peer(dy):
        return {"group": (my_y + ny + dy) % ny * CORES + core}

    barrier = pltpu.get_barrier_semaphore()

    def each(first, last, action):
        def body(k, carry):
            action(k)
            return carry

        lax.fori_loop(first, last, body, 0)

    def greet(device):
        pl.semaphore_signal(barrier, inc=1, device_id=device, device_id_type=MESH)

    each(1, slabs, lambda k: greet(server(k, 1)))
    for dy in range(1, ny):
        each(0, nx * CORES, lambda i: greet(plane_at(i // CORES, dy, i % CORES)))
    greet(at(0, nz // 2, 0))
    greeted = slabs - 1 + (ny - 1) * nx * CORES + 1

    def half_copy(p):
        return pltpu.make_async_remote_copy(
            src_ref=vol_ref.at[my_y * PARTS + p], dst_ref=held.at[my_y * PARTS + p],
            send_sem=half_ss.at[p], recv_sem=half_rs.at[p], device_id=at(0, nz // 2, 0), device_id_type=MESH,
        )

    def share_copy(dy, p):
        i = dy * PARTS + p
        return pltpu.make_async_remote_copy(
            src_ref=held.at[my_y * PARTS + p], dst_ref=held.at[my_y * PARTS + p],
            send_sem=share_ss.at[i], recv_sem=share_rs.at[i], device_id=y_peer(dy), device_id_type=MESH,
        )

    @pl.when(core == 0)
    def _():
        held[...] = vol_ref[...]

    pl.semaphore_wait(barrier, greeted)

    @pl.when(core == 1)
    def _():
        each(0, PARTS, lambda p: half_copy(p).start())

    req = req_ref[...]
    req = jnp.concatenate([req[0:1], req[1:2]], axis=1)
    bucket, piece = req >> 10, req & 1023
    tile, slab_of = bucket % tiles, bucket // tiles
    dx = (slab_of // nz + nx - my_x) % nx
    dz = (slab_of % nz + nz - my_z) % nz
    away = (dz + nz - core * (nz // 2)) % nz
    other = ((away > near) & (away < nz - near)).astype(jnp.int32)
    away = jnp.where(other == 1, away - nz // 2, away - jnp.where(away > near, nz, 0))
    from_j = other * (2 * near + 1) + jnp.where(away > 0, 2 * away - 1, -2 * away)
    home = slab_of % nz
    dy = (home % ny + ny - my_y) % ny
    dc = (home // ny + CORES - core) % CORES
    from_k = (dx + nx * nz - from_j) % nx * nz + from_j
    to_k = (dc * ny + (dy + nx * ny - dx) % ny) * nx + dx
    both = 2 * items
    own = iota((slabs * tiles, both), 0) == slab_of * tiles + tile
    before = (iota((both, both), 0) < iota((both, both), 1)).astype(F32).astype(BF)
    earlier = mm(own.astype(F32).astype(BF), before)
    rank = jnp.sum(jnp.where(own, earlier, 0.0), axis=0, keepdims=True).astype(jnp.int32)
    seat = tile * cap + rank
    def pass_on_quarter(p):
        @pl.when(core == 1)
        def _():
            half_copy(p).wait_recv()
            for dy in range(1, ny):
                share_copy(dy, p).start()

    each(0, PARTS // 2, pass_on_quarter)
    from_spot, to_spot = from_k * chunk + seat, to_k * chunk + seat
    at_seat = iota((128, both), 0) == seat
    low = jnp.where(at_seat, (piece & 31).astype(F32), 0.0).astype(BF)
    high = jnp.where(at_seat, (piece >> 5).astype(F32), 0.0).astype(BF)
    def request_codes(step_k, out, own_in):
        chosen = (iota((slabs, both), 0) == step_k).astype(F32).astype(BF)
        codes = lax.dot_general(chosen, low, NT, preferred_element_type=F32)
        codes = codes + 32.0 * lax.dot_general(chosen, high, NT, preferred_element_type=F32)
        codes = codes.astype(jnp.int32)
        for k in range(slabs):
            out[k] = codes[k : k + 1]
        own_in[0] = codes[0:1]

    request_codes(from_k, code_out, code_in)

    def sum_copy(k):
        return pltpu.make_async_remote_copy(
            src_ref=sum_out.at[k], dst_ref=sum_in.at[k], send_sem=sum_ss.at[k], recv_sem=sum_rs.at[k],
            device_id=owner(k, 1), device_id_type=MESH,
        )

    def code_copy(k):
        return pltpu.make_async_remote_copy(
            src_ref=code_out.at[k], dst_ref=code_in.at[k], send_sem=code_ss.at[k], recv_sem=code_rs.at[k],
            device_id=server(k, 1), device_id_type=MESH,
        )

    def answer_copy(k):
        return pltpu.make_async_remote_copy(
            src_ref=send1.at[k], dst_ref=recv1.at[k], send_sem=ss1.at[k], recv_sem=rs1.at[k],
            device_id=server(k, -1), device_id_type=MESH,
        )

    def return_copy(k):
        return pltpu.make_async_remote_copy(
            src_ref=send2.at[k], dst_ref=recv2.at[k], send_sem=ss2.at[k], recv_sem=rs2.at[k],
            device_id=owner(k, 1), device_id_type=MESH,
        )

    each(1, slabs, lambda k: code_copy(k).start())

    each(PARTS // 2, PARTS, pass_on_quarter)

    @pl.when(core == 1)
    def _():
        for dy in range(1, ny):
            each(0, PARTS, lambda p: share_copy(dy, p).wait_recv())

    row_tile = iota((rows, box), 0) % chunk // cap

    def serve(b, carry):
        for c in range(per):
            k = b * per + c

            @pl.when(k > 0)
            def _():
                code_copy(k).wait_recv()

        for c in range(per):
            code = code_in[b * per + c].astype(F32)
            eye = iota((chunk, 128), 0) == iota((chunk, 128), 1)
            col = jnp.sum(jnp.where(eye, code, 0.0), axis=1, keepdims=True)
            hot[c * chunk : (c + 1) * chunk] = (iota((chunk, pieces), 1) == col.astype(jnp.int32)).astype(F32).astype(BF)
        fetched = mm(hot[...], held[...].reshape(pieces, width))
        for part in range(2):
            half = fetched[:, part * box : (part + 1) * box]
            answer = jnp.zeros((rows, box), F32)
            for t in range(tiles):
                answer = answer + mm(jnp.where(row_tile == t, half, 0.0).astype(BF), w_ref[t])
            send1[pl.ds(b * per, per), :, part * box : (part + 1) * box] = answer.astype(BF).reshape(per, chunk, box)
        for c in range(per):
            k = b * per + c

            @pl.when(k > 0)
            def _():
                answer_copy(k).start()

        return carry

    lax.fori_loop(0, BATCHES, serve, 0)
    recv1[0] = send1[0]

    request_codes(to_k, sum_out, sum_in)
    each(1, slabs, lambda k: sum_copy(k).start())

    spot0, spot1 = from_spot[:, :items], from_spot[:, items:]
    back0, back1 = to_spot[:, :items], to_spot[:, items:]
    diagonal = iota((items, items), 0) == iota((items, items), 1)
    col0 = jnp.sum(jnp.where(diagonal, spot0.astype(F32), 0.0), axis=1, keepdims=True).astype(jnp.int32)
    col1 = jnp.sum(jnp.where(diagonal, spot1.astype(F32), 0.0), axis=1, keepdims=True).astype(jnp.int32)
    for b in range(BATCHES):
        across = iota((items, rows), 1) + b * rows
        pick[b] = ((across == col0) | (across == col1)).astype(F32).astype(BF)
        down = iota((rows, items), 0) + b * rows
        place[b] = ((down == back0) | (down == back1)).astype(F32).astype(BF)

    each(1, slabs, lambda k: sum_copy(k).wait_recv())

    def code_line(b, carry):
        line = jnp.zeros((1, rows), F32)
        for c in range(per):
            eye = iota((chunk, 128), 0) == iota((chunk, 128), 1)
            col = jnp.sum(jnp.where(eye, sum_in[b * per + c].astype(F32), 0.0), axis=1, keepdims=True)
            spread = iota((chunk, rows), 0) + c * chunk == iota((chunk, rows), 1)
            line = line + jnp.sum(jnp.where(spread, col, 0.0), axis=0, keepdims=True)
        code_rows[b] = line.astype(jnp.int32)
        return carry

    lax.fori_loop(0, BATCHES, code_line, 0)

    number = iota((images, box), 0)
    shift = jnp.zeros((images, box), F32)
    for i in range(images):
        shift = jnp.where(number == i, (pose_ref[i] - POSES // 2).astype(F32), shift)
    phases = 2.0 * jnp.pi * shift * iota((images, box), 1).astype(F32) / box
    cos_table, sin_table = jnp.cos(phases), jnp.sin(phases)

    proj[...] = jnp.zeros_like(proj)

    def collect(b, carry):
        for c in range(per):
            k = b * per + c

            @pl.when(k > 0)
            def _():
                answer_copy(k).wait_recv()

        proj[...] += mm(pick[b], recv1[pl.ds(b * per, per)].reshape(rows, width))
        return carry

    lax.fori_loop(0, BATCHES, collect, 0)

    for i in range(images):
        part = slice(i * lines, (i + 1) * lines)
        real, imag = proj[part, :box], proj[part, box:]
        cos, sin = cos_table[i : i + 1], sin_table[i : i + 1]
        ctf = ctf_ref[cls_ref[i]]
        res_real = obs_ref[part, :box].astype(F32) - ctf * (real * cos - imag * sin)
        res_imag = obs_ref[part, box:].astype(F32) - ctf * (real * sin + imag * cos)
        res_ref[part, :box] = res_real.astype(BF)
        res_ref[part, box:] = res_imag.astype(BF)
        real, imag = ctf * res_real, ctf * res_imag
        ret[part, :box] = (real * cos + imag * sin).astype(BF)
        ret[part, box:] = (imag * cos - real * sin).astype(BF)

    def give_back(b, carry):
        filled = mm(place[b], ret[...]).astype(BF)
        send2[pl.ds(b * per, per)] = filled.reshape(per, chunk, width)
        for c in range(per):
            k = b * per + c

            @pl.when(k > 0)
            def _():
                return_copy(k).start()

        return carry

    lax.fori_loop(0, BATCHES, give_back, 0)
    recv2[0] = send2[0]
    total[...] = jnp.zeros_like(total)

    def add_parts(b, g):
        at_piece = iota((rows_added, rows), 0) + g * rows_added == code_rows[b]
        more = mm(at_piece.astype(F32).astype(BF), rows_back[...])
        total[pl.ds(g * TOGETHER, TOGETHER)] += more.reshape(TOGETHER, sum_rows, width)

    def absorb(b, carry):
        for c in range(per):
            k = b * per + c

            @pl.when(k > 0)
            def _():
                return_copy(k).wait_recv()

        got = recv2[pl.ds(b * per, per)].reshape(rows, width).astype(F32)
        for part in range(2):
            half = got[:, part * box : (part + 1) * box]
            back = jnp.zeros((rows, box), F32)
            for t in range(tiles):
                masked = jnp.where(row_tile == t, half, 0.0).astype(BF)
                back = back + lax.dot_general(masked, w_ref[t], NT, preferred_element_type=F32)
            rows_back[:, part * box : (part + 1) * box] = back.astype(BF)

        @pl.when(b < BATCHES - 1)
        def _():
            each(0, STEPS // TOGETHER, lambda g: add_parts(b, g))

        return carry

    lax.fori_loop(0, BATCHES, absorb, 0)

    root_y, root_core = my_z % ny, my_z // ny
    turn = (my_y + ny - root_y) % ny
    on_core = core == root_core
    last = BATCHES - 1
    half = nz // 2
    hops = (my_z + nz - my_y - ny * core) % nz
    way = 1 - 2 * (hops // (half + 1))
    tip = (hops == half) | (hops == half + 1)

    def chain_copy(p):
        return pltpu.make_async_remote_copy(
            src_ref=chain_out.at[p], dst_ref=chain_in.at[p], send_sem=chain_ss.at[p], recv_sem=chain_rs.at[p],
            device_id=z_peer(-way), device_id_type=MESH,
        )

    def root_copy(p):
        return pltpu.make_async_remote_copy(
            src_ref=chain_out.at[p], dst_ref=root_in.at[p], send_sem=chain_ss.at[p], recv_sem=root_rs.at[p],
            device_id=z_peer(1), device_id_type=MESH,
        )

    def y_copy(p, d, sem):
        return pltpu.make_async_remote_copy(
            src_ref=result.at[p], dst_ref=result.at[p], send_sem=sem.at[p], recv_sem=y_rs.at[p],
            device_id=y_peer(d), device_id_type=MESH,
        )

    def sibling_copy(p):
        return pltpu.make_async_remote_copy(
            src_ref=result.at[p], dst_ref=result.at[p], send_sem=sib_ss.at[p], recv_sem=sib_rs.at[p],
            device_id=sibling, device_id_type=MESH,
        )

    def goes_up(p):
        return on_core & ((turn == 0) | ((turn == 1) & (p % 2 == 0))) if ny > 2 else on_core & (turn == 0)

    def goes_down(p):
        return on_core & ((turn == 0) | ((turn == ny - 1) & (p % 2 == 1)))

    def pass_on(p):
        @pl.when(goes_up(p))
        def _():
            y_copy(p, 1, up_ss).start()

        if ny > 2:
            @pl.when(goes_down(p))
            def _():
                y_copy(p, -1, down_ss).start()

        @pl.when(on_core)
        def _():
            sibling_copy(p).start()

        back_ref[p] = result[p]

    def gather_sum(p):
        @pl.when(p % TOGETHER == 0)
        def _():
            add_parts(last, p // TOGETHER)

        @pl.when(jnp.logical_not(tip))
        def _():
            chain_copy(p).wait_recv()
            total[p] += chain_in[p].astype(F32)

        @pl.when(hops == 0)
        def _():
            root_copy(p).wait_recv()
            result[p] = (total[p] + root_in[p].astype(F32)).astype(BF)
            pass_on(p)

        @pl.when(hops > 0)
        def _():
            chain_out[p] = total[p].astype(BF)

        @pl.when((hops > 0) & (hops < nz - 1))
        def _():
            chain_copy(p).start()

        @pl.when(hops == nz - 1)
        def _():
            root_copy(p).start()

    def take_result(p):
        @pl.when(on_core & (turn > 0))
        def _():
            y_copy(p, 1, up_ss).wait_recv()
            pass_on(p)

        @pl.when(jnp.logical_not(on_core))
        def _():
            sibling_copy(p).wait_recv()
            pass_on(p)

    def sum_step(i):
        @pl.when(i < STEPS)
        def _():
            gather_sum(i)

        @pl.when(i >= STEPS)
        def _():
            take_result(i - STEPS)

    each(0, STEPS + STEPS, sum_step)

    def drain(k):
        code_copy(k).wait_send()
        sum_copy(k).wait_send()
        answer_copy(k).wait_send()
        return_copy(k).wait_send()

    def drain_step(p):
        @pl.when(hops > 0)
        def _():
            chain_copy(p).wait_send()

        @pl.when(goes_up(p))
        def _():
            y_copy(p, 1, up_ss).wait_send()

        if ny > 2:
            @pl.when(goes_down(p))
            def _():
                y_copy(p, -1, down_ss).wait_send()

        @pl.when(on_core)
        def _():
            sibling_copy(p).wait_send()

    each(1, slabs, drain)

    @pl.when(core == 1)
    def _():
        each(0, PARTS, lambda p: half_copy(p).wait_send())
        for dy in range(1, ny):
            each(0, PARTS, lambda p: share_copy(dy, p).wait_send())

    each(0, STEPS, drain_step)


def on_device(nx, nz, ny, volume, weight_tiles, ctf_table, observed, routes, piece_index, pose_index, ctf_class):
    pieces, _, box = volume.shape
    images, lines = observed.shape[:2]
    items = images * lines
    tiles = weight_tiles.shape[0]
    slabs = nx * nz
    cap = max(2, 4 * items // (slabs * tiles))
    per = slabs // BATCHES
    chunk = tiles * cap
    rows = per * chunk
    width = 2 * box
    sums = (STEPS, pieces // STEPS, width)
    parts = (ny * PARTS, pieces // (ny * PARTS), width)
    requests = (routes * 1024 + piece_index).transpose(2, 0, 1).reshape(2, items)
    vmem, smem = pl.BlockSpec(memory_space=pltpu.VMEM), pl.BlockSpec(memory_space=pltpu.SMEM)
    dma = pltpu.SemaphoreType.DMA
    back, residual = pl.pallas_call(
        functools.partial(kernel, (nx, nz, ny, tiles, cap, lines)),
        out_shape=(jax.ShapeDtypeStruct(sums, BF), jax.ShapeDtypeStruct((items, width), BF)),
        in_specs=[smem, smem, vmem, vmem, vmem, vmem, vmem],
        out_specs=(vmem, vmem),
        scratch_shapes=[
            pltpu.VMEM(parts, BF),
            *[pltpu.VMEM((slabs, 1, 128), jnp.int32)] * 4,
            pltpu.VMEM((BATCHES, 1, rows), jnp.int32),
            pltpu.VMEM((rows, pieces), BF),
            pltpu.VMEM((slabs, chunk, width), BF),
            pltpu.VMEM((slabs, chunk, width), BF),
            pltpu.VMEM((BATCHES, items, rows), BF),
            pltpu.VMEM((BATCHES, rows, items), BF),
            pltpu.VMEM((items, width), F32),
            pltpu.VMEM((items, width), BF),
            pltpu.VMEM((slabs, chunk, width), BF),
            pltpu.VMEM((slabs, chunk, width), BF),
            pltpu.VMEM((rows, width), BF),
            pltpu.VMEM(sums, F32),
            *[pltpu.VMEM(sums, BF)] * 4,
            *[dma((PARTS,))] * 2,
            *[dma((ny * PARTS,))] * 2,
            *[dma((slabs,))] * 8,
            *[dma((STEPS,))] * 8,
        ],
        compiler_params=pltpu.CompilerParams(collective_id=0, has_side_effects=True, vmem_limit_bytes=56 * 2**20),
    )(
        pose_index, ctf_class, requests, volume.reshape(parts), weight_tiles, ctf_table,
        observed.reshape(items, width),
    )
    return back.reshape(pieces, 2, box).astype(F32), residual.reshape(images, lines, 2, box)


def solution(mesh):
    slabs, groups = mesh.shape["slab"], mesh.shape["group"]
    nz = groups
    by_device = ("group", "slab")
    return jax.shard_map(
        functools.partial(on_device, slabs // nz, nz, groups // CORES),
        mesh=mesh,
        in_specs=(
            P("slab", None, None), P(), P(), P(by_device, None, None, None), P(by_device, None, None),
            P(by_device, None, None), P(by_device), P(by_device),
        ),
        out_specs=(P("slab", None, None), P(by_device, None, None, None)),
        check_vma=False,
    )
```

time: 171 us -> 159 us (0.930)
  the two profiles are of different devices: /device:TPU:33 before, /device:TPU:17 now
where the time goes in v2:
time: 159 us; the launch traced here: 158 us
  Pallas kernels  142 us (89%)
  local copies, waits for them, and re-layouts  14.7 us (9%)
    pallas_call x1, Pallas kernels, on_device(): pl.pallas_call(functools.partial(kernel, (nx, nz, ny, tiles, cap, lines))...  142 us
    reshape x1, local copies, waits for them, and re-layouts, on_device(): volume.reshape(parts)  4.88 us
    convert_element_type x1, local copies, waits for them, and re-layouts, on_device(): back.reshape(pieces, 2, box).astype(F32)  4.72 us

profile of v2, /device:TPU:17, one launch (start us, length us, event | category | flops | bytes accessed | tf_op | source)
XLA Modules:
  0.0 158.4 jit_solution(6656314832136777084)
XLA Ops:
  0.6 0.7 add_bitcast_fusion
  1.4 0.7 reshape.19.req_ref
  2.0 2.0 %copy.11 = bf16[48,8,2,384]{3,1,2,0:T(8,128)(2,1)} copy(bf16[48,8,2,384]{3,2,1,0:T(2,128)(2,1)} %bitcast.6) | data formatting | bytes 1179648
  4.0 4.9 %reshape.20.vol_ref = bf16[16,64,768]{2,1,0:T(8,128)(2,1)} reshape(bf16[1024,2,384]{2,1,0:T(2,128)(2,1)} %param.8) | data formatting | bytes 3145728 | tf_op jit(solution)/shard_map/reshape | solution.py:531
  8.8 142.3 %shard_map.95 = (bf16[8,128,768]{2,1,0:T(8,128)(2,1)}, bf16[384,768]{1,0:T(8,128)(2,1)}) custom-call(s32[8]{0:T(128)} %pose_ref.1, s32[8]{0:T(128)} %cls_ref.1, s32[2,384]{1,0:T(2,128)} %reshape.19.req_ref, bf16[16,64,768]{2,1,0:T(8,128)(2,1)} %reshape.20.vol_ref, bf16[4,384,384]{2,1,0:T(8,128)(2,1)} %w_ref.1, f32[8,48,384]{2,1,0:T(8,128)} %ctf_ref.1, ...), custom_call_target="tpu_custom_call" | custom-call | tf_op jit(solution)/shard_map/pallas_call | solution.py:503
  151.1 2.5 %reshape.22 = bf16[8,48,2,384]{3,2,1,0:T(2,128)(2,1)} reshape(bf16[384,768]{1,0:T(8,128)(2,1)} %get-tuple-element.5) | data formatting | bytes 1179648 | tf_op jit(solution)/shard_map/reshape | solution.py:534
  153.6 4.7 %reshape.23 = f32[1024,2,384]{2,1,0:T(2,128)} reshape(bf16[8,128,768]{2,1,0:T(8,128)(2,1)} %get-tuple-element.4) | data formatting | bytes 4718592 | tf_op jit(solution)/shard_map/convert_element_type | solution.py:534
  (1 shorter events, 0.0 us)

commit v3 on v2

--- a/solution.py
+++ b/solution.py
@@ -31,7 +31,7 @@
     cfg,
     pose_ref, cls_ref, req_ref, vol_ref, w_ref, ctf_ref, obs_ref,
     back_ref, res_ref,
-    held, code_out, code_in, sum_out, sum_in, code_rows, hot, send1, recv1, pick, place, proj, ret, send2, recv2, rows_back, total,
+    seen, held, code_out, code_in, sum_out, sum_in, code_rows, hot, send1, recv1, pick, place, proj, ret, send2, recv2, rows_back, total,
     chain_out, chain_in, root_in, result,
     half_ss, half_rs, share_ss, share_rs, code_ss, code_rs, sum_ss, sum_rs, ss1, rs1, ss2, rs2, chain_ss, chain_rs, root_rs, up_ss, down_ss, y_rs, sib_ss, sib_rs,
 ):
@@ -118,27 +118,20 @@
     def _():
         held[...] = vol_ref[...]
 
-    pl.semaphore_wait(barrier, greeted)
-
-    @pl.when(core == 1)
-    def _():
-        each(0, PARTS, lambda p: half_copy(p).start())
-
     req = req_ref[...]
     req = jnp.concatenate([req[0:1], req[1:2]], axis=1)
     bucket, piece = req >> 10, req & 1023
-    tile, slab_of = bucket % tiles, bucket // tiles
-    dx = (slab_of // nz + nx - my_x) % nx
-    dz = (slab_of % nz + nz - my_z) % nz
-    away = (dz + nz - core * (nz // 2)) % nz
+    tile, slab_of = bucket & tiles - 1, bucket >> tiles.bit_length() - 1
+    home = slab_of & nz - 1
+    dx = (slab_of >> nz.bit_length() - 1) + nx - my_x & nx - 1
+    away = home + 2 * nz - my_z - core * (nz // 2) & nz - 1
     other = ((away > near) & (away < nz - near)).astype(jnp.int32)
     away = jnp.where(other == 1, away - nz // 2, away - jnp.where(away > near, nz, 0))
     from_j = other * (2 * near + 1) + jnp.where(away > 0, 2 * away - 1, -2 * away)
-    home = slab_of % nz
-    dy = (home % ny + ny - my_y) % ny
-    dc = (home // ny + CORES - core) % CORES
-    from_k = (dx + nx * nz - from_j) % nx * nz + from_j
-    to_k = (dc * ny + (dy + nx * ny - dx) % ny) * nx + dx
+    dy = (home & ny - 1) + ny - my_y & ny - 1
+    dc = (home >> ny.bit_length() - 1) + CORES - core & CORES - 1
+    from_k = (dx + nx * nz - from_j & nx - 1) * nz + from_j
+    to_k = (dc * ny + (dy + nx * ny - dx & ny - 1)) * nx + dx
     both = 2 * items
     own = iota((slabs * tiles, both), 0) == slab_of * tiles + tile
     before = (iota((both, both), 0) < iota((both, both), 1)).astype(F32).astype(BF)
@@ -152,7 +145,6 @@
             for dy in range(1, ny):
                 share_copy(dy, p).start()
 
-    each(0, PARTS // 2, pass_on_quarter)
     from_spot, to_spot = from_k * chunk + seat, to_k * chunk + seat
     at_seat = iota((128, both), 0) == seat
     low = jnp.where(at_seat, (piece & 31).astype(F32), 0.0).astype(BF)
@@ -167,6 +159,8 @@
         own_in[0] = codes[0:1]
 
     request_codes(from_k, code_out, code_in)
+    pl.semaphore_wait(barrier, greeted)
+
 
     def sum_copy(k):
         return pltpu.make_async_remote_copy(
@@ -194,14 +188,19 @@
 
     each(1, slabs, lambda k: code_copy(k).start())
 
-    each(PARTS // 2, PARTS, pass_on_quarter)
+    @pl.when(core == 1)
+    def _():
+        each(0, PARTS, lambda p: half_copy(p).start())
+
+    each(0, PARTS, pass_on_quarter)
 
     @pl.when(core == 1)
     def _():
         for dy in range(1, ny):
             each(0, PARTS, lambda p: share_copy(dy, p).wait_recv())
 
-    row_tile = iota((rows, box), 0) % chunk // cap
+    row_tile = sum((iota((per, chunk, box), 1) >= t * cap).astype(jnp.int32) for t in range(1, tiles))
+    row_tile = row_tile.reshape(rows, box)
 
     def serve(b, carry):
         for c in range(per):
@@ -271,6 +270,10 @@
     cos_table, sin_table = jnp.cos(phases), jnp.sin(phases)
 
     proj[...] = jnp.zeros_like(proj)
+    for i in range(images):
+        part = slice(i * lines, (i + 1) * lines)
+        both_parts = obs_ref[part].astype(F32)
+        seen[part, :box], seen[part, box:] = both_parts[:, 0].astype(BF), both_parts[:, 1].astype(BF)
 
     def collect(b, carry):
         for c in range(per):
@@ -290,10 +293,9 @@
         real, imag = proj[part, :box], proj[part, box:]
         cos, sin = cos_table[i : i + 1], sin_table[i : i + 1]
         ctf = ctf_ref[cls_ref[i]]
-        res_real = obs_ref[part, :box].astype(F32) - ctf * (real * cos - imag * sin)
-        res_imag = obs_ref[part, box:].astype(F32) - ctf * (real * sin + imag * cos)
-        res_ref[part, :box] = res_real.astype(BF)
-        res_ref[part, box:] = res_imag.astype(BF)
+        res_real = seen[part, :box].astype(F32) - ctf * (real * cos - imag * sin)
+        res_imag = seen[part, box:].astype(F32) - ctf * (real * sin + imag * cos)
+        seen[part, :box], seen[part, box:] = res_real.astype(BF), res_imag.astype(BF)
         real, imag = ctf * res_real, ctf * res_imag
         ret[part, :box] = (real * cos + imag * sin).astype(BF)
         ret[part, box:] = (imag * cos - real * sin).astype(BF)
@@ -313,6 +315,10 @@
     lax.fori_loop(0, BATCHES, give_back, 0)
     recv2[0] = send2[0]
     total[...] = jnp.zeros_like(total)
+    for i in range(images):
+        part = slice(i * lines, (i + 1) * lines)
+        both_parts = jnp.stack([seen[part, :box].astype(F32), seen[part, box:].astype(F32)], axis=1)
+        res_ref[part] = both_parts.astype(BF)
 
     def add_parts(b, g):
         at_piece = iota((rows_added, rows), 0) + g * rows_added == code_rows[b]
@@ -502,10 +508,11 @@
     dma = pltpu.SemaphoreType.DMA
     back, residual = pl.pallas_call(
         functools.partial(kernel, (nx, nz, ny, tiles, cap, lines)),
-        out_shape=(jax.ShapeDtypeStruct(sums, BF), jax.ShapeDtypeStruct((items, width), BF)),
+        out_shape=(jax.ShapeDtypeStruct(sums, BF), jax.ShapeDtypeStruct((items, 2, box), BF)),
         in_specs=[smem, smem, vmem, vmem, vmem, vmem, vmem],
         out_specs=(vmem, vmem),
         scratch_shapes=[
+            pltpu.VMEM((items, width), BF),
             pltpu.VMEM(parts, BF),
             *[pltpu.VMEM((slabs, 1, 128), jnp.int32)] * 4,
             pltpu.VMEM((BATCHES, 1, rows), jnp.int32),
@@ -529,7 +536,7 @@
         compiler_params=pltpu.CompilerParams(collective_id=0, has_side_effects=True, vmem_limit_bytes=56 * 2**20),
     )(
         pose_index, ctf_class, requests, volume.reshape(parts), weight_tiles, ctf_table,
-        observed.reshape(items, width),
+        observed.reshape(items, 2, box),
     )
     return back.reshape(pieces, 2, box).astype(F32), residual.reshape(images, lines, 2, box)
 

time: 159 us -> 151 us (0.950)
  Pallas kernels: 142 us -> 138 us
  local copies, waits for them, and re-layouts: 14.7 us -> 11.2 us
    pallas_call x1, Pallas kernels: 142 us -> 138 us  [on_device(): pl.pallas_call(functools.partial(kernel, (nx, nz, ny, tiles, cap, lines))...]
    reshape x1 -> x0, local copies, waits for them, and re-layouts: 2.5 us -> none  [on_device(): residual.reshape(images, lines, 2, box)]
where the time goes in v3:
time: 151 us; the launch traced here: 150 us
  Pallas kernels  138 us (91%)
  local copies, waits for them, and re-layouts  11.2 us (7%)
    pallas_call x1, Pallas kernels, on_device(): pl.pallas_call(functools.partial(kernel, (nx, nz, ny, tiles, cap, lines))...  138 us
    reshape x1, local copies, waits for them, and re-layouts, on_device(): volume.reshape(parts)  4.88 us
    convert_element_type x1, local copies, waits for them, and re-layouts, on_device(): back.reshape(pieces, 2, box).astype(F32)  4.79 us

profile of v3, /device:TPU:17, one launch (start us, length us, event | category | flops | bytes accessed | tf_op | source)
XLA Modules:
  0.0 150.4 jit_solution(574273511227170706)
XLA Ops:
  0.6 0.7 add_bitcast_fusion
  1.4 0.7 reshape.19.req_ref
  2.0 4.9 %reshape.20.vol_ref = bf16[16,64,768]{2,1,0:T(8,128)(2,1)} reshape(bf16[1024,2,384]{2,1,0:T(2,128)(2,1)} %param.8) | data formatting | bytes 3145728 | tf_op jit(solution)/shard_map/reshape | solution.py:538
  6.9 137.9 %shard_map.95 = (bf16[8,128,768]{2,1,0:T(8,128)(2,1)}, bf16[384,2,384]{2,1,0:T(2,128)(2,1)}) custom-call(s32[8]{0:T(128)} %pose_ref.1, s32[8]{0:T(128)} %cls_ref.1, s32[2,384]{1,0:T(2,128)} %reshape.19.req_ref, bf16[16,64,768]{2,1,0:T(8,128)(2,1)} %reshape.20.vol_ref, bf16[4,384,384]{2,1,0:T(8,128)(2,1)} %w_ref.1, f32[8,48,384]{2,1,0:T(8,128)} %ctf_ref.1, ...), custom_call_target="tpu_custom_call" | custom-call | tf_op jit(solution)/shard_map/pallas_call | solution.py:509
  144.8 0.0 copy-start
  144.8 4.8 %reshape.23 = f32[1024,2,384]{2,1,0:T(2,128)} reshape(bf16[8,128,768]{2,1,0:T(8,128)(2,1)} %get-tuple-element.4) | data formatting | bytes 4718592 | tf_op jit(solution)/shard_map/convert_element_type | solution.py:541
  149.6 0.0 copy-done
  149.6 0.8 copy.12
  (1 shorter events, 0.0 us)
Async XLA Ops:
  144.8 4.8 %copy-start = (bf16[384,2,384]{2,1,0:T(2,128)(2,1)S(1)}, bf16[384,2,384]{2,1,0:T(2,128)(2,1)}, u32[]{:S(2)}) copy-start(bf16[384,2,384]{2,1,0:T(2,128)(2,1)} %get-tuple-element.5) | copy-start | bytes 1769476

commit v4 on v3

--- a/solution.py
+++ b/solution.py
@@ -14,6 +14,7 @@
 PARTS = 4
 STEPS = 8
 TOGETHER = 2
+LAG = 8
 BF = jnp.bfloat16
 F32 = jnp.float32
 NT = (((1,), (1,)), ((), ()))
@@ -41,8 +42,8 @@
     chunk = tiles * cap
     rows = per * chunk
     items = req_ref.shape[1]
-    part_rows, width = vol_ref.shape[1:]
-    pieces = ny * PARTS * part_rows
+    pieces, width = vol_ref.shape
+    part_rows = pieces // (ny * PARTS)
     box = width // 2
     sum_rows = pieces // STEPS
     rows_added = TOGETHER * sum_rows
@@ -103,7 +104,8 @@
 
     def half_copy(p):
         return pltpu.make_async_remote_copy(
-            src_ref=vol_ref.at[my_y * PARTS + p], dst_ref=held.at[my_y * PARTS + p],
+            src_ref=vol_ref.at[pl.ds(pl.multiple_of((my_y * PARTS + p) * part_rows, part_rows), part_rows)],
+            dst_ref=held.at[my_y * PARTS + p],
             send_sem=half_ss.at[p], recv_sem=half_rs.at[p], device_id=at(0, nz // 2, 0), device_id_type=MESH,
         )
 
@@ -116,7 +118,7 @@
 
     @pl.when(core == 0)
     def _():
-        held[...] = vol_ref[...]
+        held[...] = vol_ref[...].reshape(held.shape)
 
     req = req_ref[...]
     req = jnp.concatenate([req[0:1], req[1:2]], axis=1)
@@ -403,7 +405,9 @@
         def _():
             sibling_copy(p).start()
 
-        back_ref[p] = result[p]
+        done = result[p].astype(F32)
+        done = jnp.stack([done[:, :box], done[:, box:]], axis=1)
+        back_ref[pl.ds(p * sum_rows, sum_rows)] = done.astype(BF)
 
     def gather_sum(p):
         @pl.when(p % TOGETHER == 0)
@@ -449,11 +453,11 @@
         def _():
             gather_sum(i)
 
-        @pl.when(i >= STEPS)
-        def _():
-            take_result(i - STEPS)
-
-    each(0, STEPS + STEPS, sum_step)
+        @pl.when(i >= LAG)
+        def _():
+            take_result(i - LAG)
+
+    each(0, STEPS + LAG, sum_step)
 
     def drain(k):
         code_copy(k).wait_send()
@@ -508,7 +512,7 @@
     dma = pltpu.SemaphoreType.DMA
     back, residual = pl.pallas_call(
         functools.partial(kernel, (nx, nz, ny, tiles, cap, lines)),
-        out_shape=(jax.ShapeDtypeStruct(sums, BF), jax.ShapeDtypeStruct((items, 2, box), BF)),
+        out_shape=(jax.ShapeDtypeStruct((pieces, 2, box), BF), jax.ShapeDtypeStruct((items, 2, box), BF)),
         in_specs=[smem, smem, vmem, vmem, vmem, vmem, vmem],
         out_specs=(vmem, vmem),
         scratch_shapes=[
@@ -535,10 +539,10 @@
         ],
         compiler_params=pltpu.CompilerParams(collective_id=0, has_side_effects=True, vmem_limit_bytes=56 * 2**20),
     )(
-        pose_index, ctf_class, requests, volume.reshape(parts), weight_tiles, ctf_table,
+        pose_index, ctf_class, requests, volume.reshape(pieces, width), weight_tiles, ctf_table,
         observed.reshape(items, 2, box),
     )
-    return back.reshape(pieces, 2, box).astype(F32), residual.reshape(images, lines, 2, box)
+    return back.astype(F32), residual.reshape(images, lines, 2, box)
 
 
 def solution(mesh):

time: 151 us -> 148 us (0.980)
  local copies, waits for them, and re-layouts: 11.2 us -> 4.35 us
  other arithmetic: 0.72 us -> 4.93 us
    reshape x1 -> x0, local copies, waits for them, and re-layouts: 4.88 us -> none  [on_device(): volume.reshape(parts)]
    convert_element_type x1 -> x0, local copies, waits for them, and re-layouts: 4.79 us -> none  [on_device(): back.reshape(pieces, 2, box).astype(F32)]
    convert_element_type x0 -> x1, other arithmetic: none -> 4.21 us  [on_device(): return (back.astype(F32), residual.reshape(images, lines, 2, box))]
    unnamed x3 -> x4, local copies, waits for them, and re-layouts: 0.82 us -> 3.68 us
where the time goes in v4:
time: 148 us
  Pallas kernels  138 us (93%)
  other arithmetic  4.93 us (3%)
  local copies, waits for them, and re-layouts  4.35 us (3%)
    pallas_call x1, Pallas kernels, on_device(): pl.pallas_call(functools.partial(kernel, (nx, nz, ny, tiles, cap, lines))...  138 us
    convert_element_type x1, other arithmetic, on_device(): return (back.astype(F32), residual.reshape(images, lines, 2, box))  4.21 us
    unnamed x4, local copies, waits for them, and re-layouts  3.68 us

profile of v4, /device:TPU:17, one launch (start us, length us, event | category | flops | bytes accessed | tf_op | source)
XLA Modules:
  0.0 148.0 jit_solution(15731236311858330740)
XLA Ops:
  0.6 0.7 add_bitcast_fusion
  1.4 0.7 reshape.16.req_ref
  2.0 2.9 %copy.11 = bf16[128,8,2,384]{3,1,2,0:T(8,128)(2,1)} copy(bf16[128,8,2,384]{3,2,1,0:T(2,128)(2,1)} %bitcast.7) | data formatting | bytes 3145728
  4.9 138.1 %shard_map.95 = (bf16[1024,2,384]{2,1,0:T(2,128)(2,1)}, bf16[384,2,384]{2,1,0:T(2,128)(2,1)}) custom-call(s32[8]{0:T(128)} %pose_ref.1, s32[8]{0:T(128)} %cls_ref.1, s32[2,384]{1,0:T(2,128)} %reshape.16.req_ref, bf16[1024,768]{1,0:T(8,128)(2,1)} %bitcast.6, bf16[4,384,384]{2,1,0:T(8,128)(2,1)} %w_ref.1, f32[8,48,384]{2,1,0:T(8,128)} %ctf_ref.1, ...), custom_call_target="tpu_custom_call" | custom-call | tf_op jit(solution)/shard_map/pallas_call | solution.py:513
  143.0 0.0 copy-start
  143.0 4.2 %convert_element_type.3 = f32[1024,2,384]{2,1,0:T(2,128)} convert(bf16[1024,2,384]{2,1,0:T(2,128)(2,1)} %get-tuple-element.4) | non-fusion elementwise | flops 786432 | bytes 4718592 | tf_op jit(solution)/shard_map/convert_element_type | solution.py:545
  147.2 0.0 copy-done
  147.2 0.8 copy.13
  (1 shorter events, 0.0 us)
Async XLA Ops:
  143.0 4.2 %copy-start = (bf16[384,2,384]{2,1,0:T(2,128)(2,1)S(1)}, bf16[384,2,384]{2,1,0:T(2,128)(2,1)}, u32[]{:S(2)}) copy-start(bf16[384,2,384]{2,1,0:T(2,128)(2,1)} %get-tuple-element.5) | copy-start | bytes 1769476
